TPU v7x, 128 devices: a whole 4x4x4 slice. The times are simulated.
128 devices in a mesh: basis: 16 (over z, y_hi, core), aux: 8 (over x, y_lo).
Axes of the slice: x: 4, y: 4 (y_hi: 2, y_lo: 2; y = y_hi * 2 + y_lo), z: 4, core: 2. Of those that a mesh axis runs over, the one named last changes fastest.
Arguments:
- three_index: bfloat16 [1536, 16, 8192], P('aux', None, 'basis'), may hold values from -0.47851562 to 0.47851562
Outputs:
- exchange: float32 [8192, 8192], P(('basis', 'aux'))
All inputs are finite; a program needn't handle non-finite values.
Results may differ from a plain program's by a relative error of at most 0.0003.
Values may be sent and summed in bfloat16 or wider, within the bound.
A program may use at most 192 MiB of HBM per device.

v0:
```python
import jax
import jax.numpy as jnp
from jax import lax
from jax.experimental import pallas as pl
from jax.experimental.pallas import tpu as pltpu
from jax.sharding import PartitionSpec as P

MESH = pl.DeviceIdType.MESH


def position():
    b = lax.axis_index("basis")
    a = lax.axis_index("aux")
    return b // 4, (b // 2) % 2, b % 2, a // 2, a % 2


def device(z, h, c, x, l):
    return (z * 4 + h * 2 + c, x * 2 + l)


def remote(src, dst, send, recv, who):
    return pltpu.make_async_remote_copy(
        src_ref=src, dst_ref=dst, send_sem=send, recv_sem=recv,
        device_id=who, device_id_type=MESH,
    )


LEVELS = 10
SPREAD = 256.0 * LEVELS


def encode(value, ref):
    rest = []
    for k in range(2):
        one = value[32 * k : 32 * k + 32]
        high = one.astype(jnp.bfloat16)
        ref[32 * k : 32 * k + 32] = high
        high = high.astype(jnp.float32)
        scale = SPREAD * pl.reciprocal(jnp.maximum(jnp.abs(high), 1e-30), approx=True)
        rest.append(jnp.floor((one - high) * scale + 0.5))
    ref[64:96] = (rest[0] * (2 * LEVELS + 1) + rest[1]).astype(jnp.bfloat16)


def decode(ref):
    both = ref[64:96].astype(jnp.float32)
    first = jnp.floor(both * (1.0 / (2 * LEVELS + 1)) + 0.5)
    out = []
    for k, rest in enumerate((first, both - first * (2 * LEVELS + 1))):
        high = ref[32 * k : 32 * k + 32].astype(jnp.float32)
        out.append(high + jnp.abs(high) * (rest * (1.0 / SPREAD)))
    return jnp.concatenate(out, axis=0)


def kernel(a_ref, out_ref, stage, rows, cols, hop, part, put1, put2, got1, got2, done, turned, packed, byrow, bycol,
           bits, ls, ss, rs, s1, r1, s2, r2, sr, rr, st, rt):
    z, h, c, x, l = position()
    m = 1 - l
    mate = device(z, h, c, x, m)
    other = device(z, 1 - h, c, x, m)
    cross = device(z, 1 - h, c, x, l)
    core = device(z, h, 1 - c, x, l)
    down = device((z + 3) % 4, h, c, x, l)
    up = device((z + 1) % 4, h, c, x, l)
    xa = x + 1 - 2 * (x % 2)
    xb = 3 - x
    xo = 3 - xa
    near_a = device(z, h, c, xa, l)
    near_b = device(z, h, c, xb, l)
    depth = a_ref.shape[0]
    half = rows.shape[3]
    quarter = depth // 4

    barrier = pltpu.get_barrier_semaphore()
    senders = [mate, other, cross, core, up, near_a, near_b]
    for i in (1, 2):
        for cs in range(2):
            for xs in range(4):
                senders.append(device((z + 4 - i) % 4, h, cs, xs, l))
    for who in senders:
        pl.semaphore_signal(barrier, inc=1, device_id=who, device_id_type=MESH)

    loads = [
        pltpu.make_async_copy(
            a_ref.at[pl.ds(q * quarter, quarter)], stage.at[pl.ds(q * quarter, quarter)], ls.at[q]
        )
        for q in range(4)
    ]
    for one in loads:
        one.start()
    def sort(q):
        loads[q].wait()

        def body(n, carry):
            at = pl.multiple_of(q * quarter + n * 128, 128)
            block = stage[pl.ds(at, 128), :]
            for g in range(2):
                rows[0, g, pl.ds(at, 128), :] = jnp.concatenate(
                    [block[:, t * 128 + g * 64 : t * 128 + g * 64 + 64] for t in range(4)], axis=1
                )
            return carry

        lax.fori_loop(0, quarter // 128, body, 0)

    fours = [(q * quarter, quarter) for q in range(4)]
    parts = [(0, 2 * quarter), (2 * quarter, quarter), (3 * quarter, quarter)]

    def copies(n, src, dst, who, spans):
        return [
            remote(src.at[pl.ds(*span)], dst.at[pl.ds(*span)], ss.at[n, k], rs.at[n, k], who)
            for k, span in enumerate(spans)
        ]

    def side(n, cr):
        return cols.at[n, :, pl.ds(cr * half, half)]

    whole = [(0, depth)]
    mate1 = copies(0, rows.at[0, m], rows.at[1, m], mate, fours)
    mate2 = copies(1, rows.at[0, l], rows.at[1, l], mate, whole)
    relay2 = copies(2, rows.at[3, m], rows.at[2, m], mate, parts)
    other1 = copies(3, rows.at[0, l], rows.at[3, l], other, fours)
    relay1 = copies(4, rows.at[1, l], rows.at[2, l], other, fours)
    other2 = copies(5, rows.at[0, m], rows.at[3, m], other, parts)
    down1 = copies(6, rows.at[0, l], side(2 + l, 0), down, whole)
    down2 = copies(7, rows.at[1, l], side(2 + m, 0), down, fours)
    core1 = copies(8, rows.at[0, l], side(l, 1), core, whole)
    core2 = copies(9, rows.at[1, l], side(m, 1), core, fours)
    core3 = copies(10, side(2 + l, 0), side(2 + l, 1), core, whole)
    core4 = copies(11, side(2 + m, 0), side(2 + m, 1), core, fours)
    core5 = copies(12, side(4, 0), side(4, 1), core, fours)
    take = ((z + 2) % 4) // 2
    soon = take == l
    relay_soon = ((z + 1) % 4) // 2 == l
    lift = copies(13, rows.at[(take + l) % 2, l], hop, up, fours)
    forward = copies(14, hop, side(4, 0), up, fours)
    keep1 = pltpu.make_async_copy(rows.at[0, l], side(l, 0), ls.at[4])
    keep2 = pltpu.make_async_copy(rows.at[1, l], side(m, 0), ls.at[5])
    core6 = copies(15, rows.at[0, m], side(5, 1), core, whole)
    core7 = copies(16, rows.at[1, m], side(6, 1), core, whole)
    keep3 = pltpu.make_async_copy(rows.at[0, m], side(5, 0), ls.at[6])
    keep4 = pltpu.make_async_copy(rows.at[1, m], side(6, 0), ls.at[7])

    def start(those):
        for one in those:
            one.start()

    def arrive(those):
        for one in those:
            one.wait_recv()

    def pass_on(k):
        lift[k].wait_recv()
        forward[k].start()

    def multiply(i, hr, role, g, column, first, k=None, to=None):
        span = pl.ds(0, depth) if k is None else pl.ds(*parts[k])
        block = lax.dot_general(
            rows[role, g, span], cols[column, span], (((0,), (0,)), ((), ())),
            preferred_element_type=jnp.float32,
        )
        for cr in range(2):
            piece = block[:, cr * half : cr * half + half].reshape(4, 64, half)
            if first:
                part[i, hr, g if to is None else to, cr] = piece
            else:
                part[i, hr, g if to is None else to, cr] += piece

    def scatter1(i, hr, g):
        return [
            remote(
                put1.at[i, hr, g, cr, k], got1.at[i, hr, g, cr, k],
                s1.at[i, hr, g, cr, k], r1.at[i, hr, g, cr, k], near,
            )
            for cr, near in ((0, near_a), (1, near_b))
            for k in range(2)
        ]

    def scatter2(i, hr, g):
        return [
            remote(
                put2.at[i, hr, g, cr], got2.at[i, hr, g, cr],
                s2.at[i, hr, g, cr], r2.at[i, hr, g, cr], near,
            )
            for cr, near in ((0, near_b), (1, near_a))
        ]

    def begin(i, hr, g):
        for cr, mine in ((0, xa), (1, xb)):
            for k, piece in ((0, mine), (1, xo)):
                encode(part[i, hr, g, cr, piece], put1.at[i, hr, g, cr, k])
        for one in scatter1(i, hr, g):
            one.start()

    def middle(i, hr, g):
        for one in scatter1(i, hr, g):
            one.wait_recv()
        for cr, piece in ((0, xb), (1, xa)):
            encode(part[i, hr, g, cr, piece] + decode(got1.at[i, hr, g, cr, 1]), put2.at[i, hr, g, cr])
        for one in scatter2(i, hr, g):
            one.start()

    def finish(i, hr, g):
        for one in scatter2(i, hr, g):
            one.wait_recv()
        for cr in range(2):
            done[i, hr, cr, pl.ds(pl.multiple_of(g * 64, 64), 64), :] = (
                part[i, hr, g, cr, x] + decode(got1.at[i, hr, g, cr, 0]) + decode(got2.at[i, hr, g, cr])
            )

    def rowwise(i, hr, g, who, half_of=l):
        return remote(
            done.at[i, hr, :, pl.ds(pl.multiple_of(g * 64, 64), 64), :], byrow.at[hr, half_of, i],
            sr.at[i, hr, g], rr.at[i, hr, half_of], who,
        )

    def rowwise_diagonal():
        return rowwise(0, 1, l, other, m)

    def colwise(i):
        return [
            remote(
                turned.at[i - 1, cr, pl.ds(xs * 64, 64)], bycol.at[i - 1, c, x],
                st.at[i - 1, 0, cr, xs], rt.at[i - 1, 0, c, x],
                device((z + i) % 4, h, (c + cr) % 2, xs, l),
            )
            for cr in range(2)
            for xs in range(4)
        ]

    def colwise_half(i, g):
        return [
            remote(
                packed.at[i - 1, g, cr, xs], bits.at[i - 1, g, c, x],
                st.at[i - 1, 1 + g, cr, xs], rt.at[i - 1, 1 + g, c, x],
                device((z + i) % 4, h, (c + cr) % 2, xs, l),
            )
            for cr in range(2)
            for xs in range(4)
        ]

    def turn(i):
        for cr in range(2):
            turned[i - 1, cr] = done[i, 0, cr].T
        start(colwise(i))

    def turn_half(i, g):
        for cr in range(2):
            block = done[i, 1, cr, pl.ds(pl.multiple_of(g * 64, 64), 64), :].T
            for xs in range(4):
                packed[i - 1, g, cr, xs] = jnp.concatenate(
                    [block[xs * 64 : xs * 64 + 32], block[xs * 64 + 32 : xs * 64 + 64]], axis=1
                )
        start(colwise_half(i, g))

    late = (z // 2 + l) % 2

    for q in range(4):
        sort(q)
        if q == 0:
            pl.semaphore_wait(barrier, len(senders))
        mate1[q].start()
        other1[q].start()

        @pl.when(soon)
        def _():
            lift[q].start()

    start(down1 + core1 + mate2 + core6)
    keep1.start()
    keep3.start()

    for k in range(4):
        if k == 1:
            keep1.wait()
            arrive(core1)
            multiply(0, 0, 0, l, l, True)
        if k == 2:
            multiply(0, 0, 0, m, l, True)
        mate1[k].wait_recv()
        down2[k].start()
        relay1[k].start()
        core2[k].start()

        @pl.when(jnp.logical_not(soon))
        def _():
            lift[k].start()

        @pl.when(relay_soon)
        def _():
            pass_on(k)

    keep2.start()
    arrive(other1)
    start(relay2 + other2)
    arrive(down1)
    start(core3)
    keep2.wait()
    arrive(core2)
    multiply(0, 0, 1, l, m, False)
    begin(0, 0, l)
    multiply(0, 1, 3, m, m, True)
    arrive(core3)
    multiply(1, 0, 0, l, 2 + l, True)
    multiply(1, 0, 0, m, 2 + l, True)
    middle(0, 0, l)
    for k in range(2):
        @pl.when(jnp.logical_not(relay_soon))
        def _():
            pass_on(k)

    for k in range(3):
        down2[k].wait_recv()
        core4[k].start()
    finish(0, 0, l)

    arrive(mate2)
    keep4.start()
    start(core7)
    multiply(0, 0, 1, m, m, False)
    begin(0, 0, m)
    arrive(relay1)
    multiply(0, 1, 2, m, l, False)
    begin(0, 1, m)
    keep3.wait()
    arrive(core6)
    multiply(0, 1, 2, m, 5, True, to=l)
    down2[3].wait_recv()
    core4[3].start()
    multiply(1, 1, 2, m, 2 + l, True)

    @pl.when(jnp.logical_not(relay_soon))
    def _():
        pass_on(2)

    arrive(core4)
    multiply(1, 0, 1, l, 2 + m, False)
    begin(1, 0, l)
    multiply(1, 0, 1, m, 2 + m, False)
    begin(1, 0, m)
    multiply(1, 1, 3, m, 2 + m, False)
    begin(1, 1, m)
    keep4.wait()
    arrive(core7)
    multiply(0, 1, 3, m, 6, False, to=l)
    begin(0, 1, l)
    middle(0, 0, m)
    middle(0, 1, m)
    for k in range(2):
        forward[k].wait_recv()
        core5[k].start()

    @pl.when(jnp.logical_not(relay_soon))
    def _():
        pass_on(3)

    middle(1, 0, l)
    for k in range(2, 4):
        forward[k].wait_recv()
        core5[k].start()
    middle(1, 0, m)
    arrive(core5)
    multiply(2, 0, late, l, 4, True)
    begin(2, 0, l)
    multiply(2, 0, late, m, 4, True)
    begin(2, 0, m)
    multiply(2, 1, 2 + late, m, 4, True)
    begin(2, 1, m)
    middle(1, 1, m)
    finish(1, 0, l)
    finish(1, 0, m)
    turn(1)
    middle(0, 1, l)
    finish(1, 1, m)
    turn_half(1, m)

    for k in range(3):
        other2[k].wait_recv()
        relay2[k].wait_recv()
        multiply(1, 1, 3, l, 2 + m, k == 0, k)
        multiply(1, 1, 2, l, 2 + l, False, k)
        if k == 2:
            begin(1, 1, l)
        multiply(2, 1, 2 + late, l, 4, k == 0, k)
        if k == 0:
            finish(0, 0, m)
            finish(0, 1, m)
            middle(2, 0, l)
        if k == 1:
            middle(2, 0, m)
            finish(0, 1, l)
            middle(2, 1, m)
    begin(2, 1, l)
    rowwise(0, 0, m, mate).start()
    rowwise(0, 1, m, other).start()
    rowwise(1, 0, m, mate).start()
    rowwise(1, 1, m, other).start()
    rowwise_diagonal().start()
    finish(2, 0, l)
    finish(2, 0, m)
    rowwise(2, 0, m, mate).start()
    turn(2)
    finish(2, 1, m)
    rowwise(2, 1, m, other).start()
    turn_half(2, m)
    middle(1, 1, l)
    middle(2, 1, l)
    finish(1, 1, l)
    rowwise(1, 1, l, cross).start()
    turn_half(1, l)
    finish(2, 1, l)
    rowwise(2, 1, l, cross).start()
    turn_half(2, l)

    def place(zs, hs, cs, at):
        return pl.ds(pl.multiple_of(zs * 2048 + hs * 1024 + cs * 512 + at, 128), 128)

    for i in range(3):
        for cr in range(2):
            byrow[0, l, i, cr] = done[i, 0, cr, pl.ds(pl.multiple_of(l * 64, 64), 64), :]
    low = lax.broadcasted_iota(jnp.int32, (64, 128), 1) < 64
    for hr in range(2):
        for i in (1, 2):
            for cs in range(2):
                for xs in range(4):
                    where = place((z + 4 - i) % 4, (h + hr) % 2, cs, xs * 128)
                    if hr == 0:
                        remote(
                            bycol.at[i - 1, cs, xs], bycol.at[i - 1, cs, xs],
                            st.at[i - 1, 0, 0, 0], rt.at[i - 1, 0, cs, xs], mate,
                        ).wait_recv()
                        out_ref[:, where] = bycol[i - 1, cs, xs]
                    else:
                        for g in range(2):
                            remote(
                                bits.at[i - 1, g, cs, xs], bits.at[i - 1, g, cs, xs],
                                st.at[i - 1, 1 + g, 0, 0], rt.at[i - 1, 1 + g, cs, xs], mate,
                            ).wait_recv()
                        v0 = bits[i - 1, 0, cs, xs]
                        v1 = bits[i - 1, 1, cs, xs]
                        out_ref[0:32, where] = jnp.where(low[:32], v0, pltpu.roll(v1, 64, 1))
                        out_ref[32:64, where] = jnp.where(low[:32], pltpu.roll(v0, 64, 1), v1)
        for i in (1, 2, 0):
            for g in (m,) if hr == 0 else (0, 1):
                remote(byrow.at[hr, g, i], byrow.at[hr, g, i], sr.at[i, hr, g], rr.at[i, hr, g], mate).wait_recv()
            for cr in range(2):
                for t in range(2):
                    v0 = byrow[hr, 0, i, cr, :, t * 128 : t * 128 + 128]
                    v1 = byrow[hr, 1, i, cr, :, t * 128 : t * 128 + 128]
                    even = jnp.where(low, v0, pltpu.roll(v1, 64, 1))
                    odd = jnp.where(low, pltpu.roll(v0, 64, 1), v1)
                    for value, xs in ((even, 2 * t), (odd, 2 * t + 1)):
                        where = place((z + i) % 4, (h + hr) % 2, (c + cr) % 2, xs * 128)
                        if i == 2:
                            out_ref[:, where] += value
                        else:
                            out_ref[:, where] = value

    for one in (mate1 + mate2 + relay2 + other1 + relay1 + other2 + down1 + down2 + core1 + core2 + core3
                + core4 + core5 + core6 + core7 + lift + forward):
        one.wait_send()
    for i in range(3):
        for hr in range(2):
            for g in range(2):
                for one in scatter1(i, hr, g) + scatter2(i, hr, g):
                    one.wait_send()
                if hr == 1:
                    rowwise(i, 1, g, cross).wait_send()
            if hr == 0:
                rowwise(i, 0, m, mate).wait_send()
            if i:
                for one in colwise(i) if hr == 0 else colwise_half(i, 0) + colwise_half(i, 1):
                    one.wait_send()


def shards(three_index):
    depth = three_index.shape[0] * three_index.shape[1]
    own = three_index.reshape(depth, 512)
    dma = pltpu.SemaphoreType.DMA
    f32 = jnp.float32
    return pl.pallas_call(
        kernel,
        out_shape=jax.ShapeDtypeStruct((64, 8192), f32),
        in_specs=[pl.BlockSpec(memory_space=pl.ANY)],
        out_specs=pl.BlockSpec(memory_space=pltpu.VMEM),
        scratch_shapes=[
            pltpu.VMEM((depth, 512), jnp.bfloat16),
            pltpu.VMEM((4, 2, depth, 256), jnp.bfloat16),
            pltpu.VMEM((7, depth, 512), jnp.bfloat16),
            pltpu.VMEM((depth, 256), jnp.bfloat16),
            pltpu.VMEM((3, 2, 2, 2, 4, 64, 256), f32),
            pltpu.VMEM((3, 2, 2, 2, 2, 96, 256), jnp.bfloat16),
            pltpu.VMEM((3, 2, 2, 2, 96, 256), jnp.bfloat16),
            pltpu.VMEM((3, 2, 2, 2, 2, 96, 256), jnp.bfloat16),
            pltpu.VMEM((3, 2, 2, 2, 96, 256), jnp.bfloat16),
            pltpu.VMEM((3, 2, 2, 128, 256), f32),
            pltpu.VMEM((2, 2, 256, 128), f32),
            pltpu.VMEM((2, 2, 2, 4, 32, 128), f32),
            pltpu.VMEM((2, 2, 3, 2, 64, 256), f32),
            pltpu.VMEM((2, 2, 4, 64, 128), f32),
            pltpu.VMEM((2, 2, 2, 4, 32, 128), f32),
            dma((8,)), dma((17, 4)), dma((17, 4)),
            dma((3, 2, 2, 2, 2)), dma((3, 2, 2, 2, 2)), dma((3, 2, 2, 2)), dma((3, 2, 2, 2)),
            dma((3, 2, 2)), dma((3, 2, 2)), dma((2, 3, 2, 4)), dma((2, 3, 2, 4)),
        ],
        compiler_params=pltpu.CompilerParams(
            collective_id=0, has_side_effects=True, vmem_limit_bytes=60 * 2**20
        ),
        cost_estimate=pl.CostEstimate(flops=16 * 10**9, bytes_accessed=8 * 10**6, transcendentals=0),
    )(own)


def solution(mesh):
    return jax.shard_map(
        shards,
        mesh=mesh,
        in_specs=(P("aux", None, "basis"),),
        out_specs=P(("basis", "aux"), None),
        check_vma=False,
    )
```

profile of v0, /device:TPU:1, one launch (start us, length us, event | category | flops | bytes accessed | tf_op | source)
XLA Modules:
  0.0 147.2 jit_solution(16624993745552915503)
XLA Ops:
  0.0 144.1 %shard_map.17 = f32[64,8192]{1,0:T(8,128)} custom-call(bf16[3072,512]{1,0:T(8,128)(2,1)} %bitcast.1), custom_call_target="tpu_custom_call" | custom-call | flops 16000000000 | bytes 8000000 | tf_op jit(solution)/shard_map/pallas_call | solution.py:479
  144.1 3.1 %copy.3 = f32[64,8192]{1,0:T(8,128)} copy(f32[64,8192]{1,0:T(8,128)} %shard_map.17) | data formatting | bytes 4194304
where the time goes:
time: 147 us
  Pallas kernels  144 us (98%)
  local copies, waits for them, and re-layouts  3.06 us (2%)
    pallas_call x1, Pallas kernels, shards(): pl.pallas_call(kernel, out_shape=jax.ShapeDtypeStruct((64, 8192), f32), i...  144 us
    unnamed x1, local copies, waits for them, and re-layouts  3.06 us

commit v1 on v0

--- a/solution.py
+++ b/solution.py
@@ -368,9 +368,6 @@
     finish(1, 0, l)
     finish(1, 0, m)
     turn(1)
-    middle(0, 1, l)
-    finish(1, 1, m)
-    turn_half(1, m)
 
     for k in range(3):
         other2[k].wait_recv()
@@ -385,15 +382,20 @@
             finish(0, 1, m)
             middle(2, 0, l)
         if k == 1:
+            middle(0, 1, l)
             middle(2, 0, m)
-            finish(0, 1, l)
-            middle(2, 1, m)
     begin(2, 1, l)
+    middle(2, 1, m)
+    finish(1, 1, m)
+    turn_half(1, m)
     rowwise(0, 0, m, mate).start()
     rowwise(0, 1, m, other).start()
     rowwise(1, 0, m, mate).start()
     rowwise(1, 1, m, other).start()
+    finish(0, 1, l)
     rowwise_diagonal().start()
+    middle(1, 1, l)
+    middle(2, 1, l)
     finish(2, 0, l)
     finish(2, 0, m)
     rowwise(2, 0, m, mate).start()
@@ -401,8 +403,6 @@
     finish(2, 1, m)
     rowwise(2, 1, m, other).start()
     turn_half(2, m)
-    middle(1, 1, l)
-    middle(2, 1, l)
     finish(1, 1, l)
     rowwise(1, 1, l, cross).start()
     turn_half(1, l)

time: 147 us -> 149 us (1.014)
  Pallas kernels: 144 us -> 146 us
    pallas_call x1, Pallas kernels: 144 us -> 146 us  [shards(): pl.pallas_call(kernel, out_shape=jax.ShapeDtypeStruct((64, 8192), f32), i...]
where the time goes in v1:
time: 149 us
  Pallas kernels  146 us (98%)
  local copies, waits for them, and re-layouts  3.06 us (2%)
    pallas_call x1, Pallas kernels, shards(): pl.pallas_call(kernel, out_shape=jax.ShapeDtypeStruct((64, 8192), f32), i...  146 us
    unnamed x1, local copies, waits for them, and re-layouts  3.06 us

profile of v1, /device:TPU:1, one launch (start us, length us, event | category | flops | bytes accessed | tf_op | source)
XLA Modules:
  0.0 149.3 jit_solution(5190482286393765957)
XLA Ops:
  0.0 146.2 %shard_map.17 = f32[64,8192]{1,0:T(8,128)} custom-call(bf16[3072,512]{1,0:T(8,128)(2,1)} %bitcast.1), custom_call_target="tpu_custom_call" | custom-call | flops 16000000000 | bytes 8000000 | tf_op jit(solution)/shard_map/pallas_call | solution.py:479
  146.2 3.1 %copy.3 = f32[64,8192]{1,0:T(8,128)} copy(f32[64,8192]{1,0:T(8,128)} %shard_map.17) | data formatting | bytes 4194304

commit v2 on v0

--- a/solution.py
+++ b/solution.py
@@ -187,16 +187,16 @@
         for cr, mine in ((0, xa), (1, xb)):
             for k, piece in ((0, mine), (1, xo)):
                 encode(part[i, hr, g, cr, piece], put1.at[i, hr, g, cr, k])
-        for one in scatter1(i, hr, g):
-            one.start()
+                scatter1(i, hr, g)[2 * cr + k].start()
 
     def middle(i, hr, g):
-        for one in scatter1(i, hr, g):
-            one.wait_recv()
+        first = scatter1(i, hr, g)
         for cr, piece in ((0, xb), (1, xa)):
+            first[2 * cr + 1].wait_recv()
             encode(part[i, hr, g, cr, piece] + decode(got1.at[i, hr, g, cr, 1]), put2.at[i, hr, g, cr])
-        for one in scatter2(i, hr, g):
-            one.start()
+            scatter2(i, hr, g)[cr].start()
+        for cr in range(2):
+            first[2 * cr].wait_recv()
 
     def finish(i, hr, g):
         for one in scatter2(i, hr, g):
@@ -375,6 +375,12 @@
     for k in range(3):
         other2[k].wait_recv()
         relay2[k].wait_recv()
+        if k == 2:
+            rowwise(0, 0, m, mate).start()
+            rowwise(0, 1, m, other).start()
+            rowwise(1, 0, m, mate).start()
+            rowwise(1, 1, m, other).start()
+            rowwise_diagonal().start()
         multiply(1, 1, 3, l, 2 + m, k == 0, k)
         multiply(1, 1, 2, l, 2 + l, False, k)
         if k == 2:
@@ -389,11 +395,6 @@
             finish(0, 1, l)
             middle(2, 1, m)
     begin(2, 1, l)
-    rowwise(0, 0, m, mate).start()
-    rowwise(0, 1, m, other).start()
-    rowwise(1, 0, m, mate).start()
-    rowwise(1, 1, m, other).start()
-    rowwise_diagonal().start()
     finish(2, 0, l)
     finish(2, 0, m)
     rowwise(2, 0, m, mate).start()

time: 147 us -> 147 us (level)
  no operation moved by 1% of the time
where the time goes in v2:
time: 147 us
  Pallas kernels  144 us (98%)
  local copies, waits for them, and re-layouts  3.06 us (2%)
    pallas_call x1, Pallas kernels, shards(): pl.pallas_call(kernel, out_shape=jax.ShapeDtypeStruct((64, 8192), f32), i...  144 us
    unnamed x1, local copies, waits for them, and re-layouts  3.06 us

profile of v2, /device:TPU:1, one launch (start us, length us, event | category | flops | bytes accessed | tf_op | source)
XLA Modules:
  0.0 147.3 jit_solution(4904957287448357889)
XLA Ops:
  0.0 144.2 %shard_map.17 = f32[64,8192]{1,0:T(8,128)} custom-call(bf16[3072,512]{1,0:T(8,128)(2,1)} %bitcast.1), custom_call_target="tpu_custom_call" | custom-call | flops 16000000000 | bytes 8000000 | tf_op jit(solution)/shard_map/pallas_call | solution.py:480
  144.2 3.1 %copy.3 = f32[64,8192]{1,0:T(8,128)} copy(f32[64,8192]{1,0:T(8,128)} %shard_map.17) | data formatting | bytes 4194304
